TPU v7x, 32 devices: a whole 2x2x4 slice. The times are simulated.
32 devices in a mesh: seq: 16 (over z, y, core), head: 2 (over x).
Axes of the slice: x: 2, y: 2, z: 4, core: 2. Of those that a mesh axis runs over, the one named last changes fastest.
Arguments:
- queries: bfloat16 [4096, 8, 4, 128], P(('seq', 'head')), may hold values from -210 to 210
- keys: bfloat16 [4096, 8, 128], P(('seq', 'head')), may hold values from -6 to 6
- values: bfloat16 [4096, 8, 128], P(('seq', 'head')), may hold values from -6 to 6
- d_attended: bfloat16 [4096, 8, 4, 128], P(('seq', 'head')), may hold values from -12 to 12
- shift_amounts: int32 [8], replicated, may hold values from 0 to 1024, as said below
Outputs:
- attended: bfloat16 [4096, 8, 4, 128], P(('seq', 'head'))
- d_queries: bfloat16 [4096, 8, 4, 128], P(('seq', 'head'))
- d_keys: bfloat16 [4096, 8, 128], P(('seq', 'head'))
- d_values: bfloat16 [4096, 8, 128], P(('seq', 'head'))
Inputs may be any that keep to these rules, and one draw needn't show every extreme that they name: `shift_amounts`: each head's shift is 0 or 1024, and exactly half of the 8 heads have 2048 // 2.
All inputs are finite; a program needn't handle non-finite values.
Results may differ from a plain program's by a relative error of at most 0.034.
Values may be sent and summed in bfloat16 or wider, within the bound.
A program may use at most 128 MiB of HBM per device.

v0:
```python
import functools
import math

import jax
import jax.numpy as jnp
from jax import lax
from jax.experimental import pallas as pl
from jax.experimental.pallas import tpu as pltpu
from jax.sharding import PartitionSpec as P

GROUP = 2048
HALF = GROUP // 2
CHUNK = 256
MASKED = -1e30
MESH = pl.DeviceIdType.MESH


def nt(a, b):
    return lax.dot_general(a, b, (((1,), (0,)), ((), ())), preferred_element_type=jnp.float32)


def tn(a, b):
    return lax.dot_general(a, b, (((0,), (0,)), ((), ())), preferred_element_type=jnp.float32)


def kernel(
    n_seq, n_head, tok,
    shift_ref, q_ref, k_ref, v_ref, d_ref,
    o_ref, dq_ref, dk_ref, dv_ref,
    kv, part, sib, red, rb_own, rb_far, scores, o_tr, dq_tr, o_buf, dq_buf, fin, perm, inv,
    own_s, own_r, far_s, far_r, fwd_s, fwd_r, ffwd_s, ffwd_r,
    sib_s, sib_r, fsib_s, fsib_r, back_s, back_r, fback_s, fback_r,
):
    heads = k_ref.shape[0]
    near = heads // 2
    nq = q_ref.shape[1]
    span = HALF // (tok * n_head)
    rows = tok * n_head
    pairs = span // 2
    chips = pairs * n_head
    n_planes = n_seq // span
    seq = lax.axis_index("seq")
    x = lax.axis_index("head")
    plane = seq // span
    s_in = seq % span
    y = s_in // 2
    core = s_in % 2
    chip = y * n_head + x
    pos = s_in * n_head + x
    nxt = (plane + 1) % n_planes
    prv = (plane + n_planes - 1) % n_planes
    scaling = 1.0 / math.sqrt(k_ref.shape[2])
    to_exp2 = scaling * math.log2(math.e)

    def device(at_plane, at_chip):
        return (at_plane * span + (at_chip // n_head) * 2 + core, at_chip % n_head)

    sibling = (plane * span + y * 2 + 1 - core, x)

    def place(at_chip):
        return ((at_chip // n_head) * 2 + core) * n_head + at_chip % n_head

    barrier = pltpu.get_barrier_semaphore()
    pl.semaphore_signal(barrier, inc=1, device_id=sibling, device_id_type=MESH)
    for k in range(chips):
        other = (chip + k) % chips
        if k:
            pl.semaphore_signal(barrier, inc=1, device_id=device(plane, other), device_id_type=MESH)
        pl.semaphore_signal(barrier, inc=1, device_id=device(nxt, other), device_id_type=MESH)
        pl.semaphore_signal(barrier, inc=1, device_id=device(prv, other), device_id_type=MESH)

    even = plane % 2 == 0
    n_near = jnp.int32(0)
    n_far = jnp.int32(0)
    ranks = []
    for h in range(heads):
        is_near = (shift_ref[h] == 0) == even
        ranks.append(jnp.where(is_near, n_near, (near + n_far) % heads))
        n_near = n_near + is_near.astype(jnp.int32)
        n_far = n_far + 1 - is_near.astype(jnp.int32)
    for h in range(heads):
        inv[h] = ranks[h]
        perm[h] = sum(jnp.where(ranks[j] == h, j, 0) for j in range(heads))

    mine = pl.ds(pl.multiple_of(HALF + pos * tok, tok), tok)
    for i in range(heads):
        kv[i, 0, mine, :] = k_ref[perm[i]]
        kv[i, 1, mine, :] = v_ref[perm[i]]

    def remote(src, dst, ssem, rsem, dev):
        return pltpu.make_async_remote_copy(
            src_ref=src, dst_ref=dst, send_sem=ssem, recv_sem=rsem, device_id=dev, device_id_type=MESH
        )

    def own_copy(i, to):
        view = kv.at[i, :, mine, :]
        return remote(view, view, own_s.at[i, to], own_r.at[i, chip], device(plane, to))

    def own_arrival(i, source):
        view = kv.at[i, :, pl.ds(pl.multiple_of(HALF + place(source) * tok, tok), tok), :]
        return remote(view, view, own_s.at[i, source], own_r.at[i, source], device(plane, source))

    def far_copy(i, to):
        return remote(
            kv.at[i, :, mine, :],
            kv.at[i + near, :, pl.ds(pl.multiple_of(pos * tok, tok), tok), :],
            far_s.at[i, to], far_r.at[i, chip], device(nxt, to),
        )

    def far_arrival(i, source):
        view = kv.at[i, :, pl.ds(pl.multiple_of(place(source) * tok, tok), tok), :]
        return remote(view, view, far_s.at[i - near, source], far_r.at[i - near, source], device(prv, source))

    def strip(base, at_pair, parity):
        return pl.ds(pl.multiple_of(base + (at_pair * 2 + parity) * rows, rows), rows)

    def forward(i, at_pair, parity):
        view = kv.at[i, :, strip(HALF, at_pair, parity), :]
        return remote(view, view, fwd_s.at[i, at_pair], fwd_r.at[i, at_pair], sibling)

    def far_forward(i, at_pair, parity):
        view = kv.at[i, :, strip(0, at_pair, parity), :]
        return remote(view, view, ffwd_s.at[i - near, at_pair], ffwd_r.at[i - near, at_pair], sibling)

    def packed(region, at_pair):
        return pl.ds((region * pairs + at_pair) * rows, rows)

    def sib_copy(i, at_pair):
        return remote(
            part.at[i, :, strip(HALF, at_pair, 1 - core), :], sib.at[i, :, packed(1, at_pair), :],
            sib_s.at[i, at_pair], sib_r.at[i, at_pair], sibling,
        )

    def far_sib_copy(i, at_pair):
        return remote(
            part.at[i, :, strip(0, at_pair, 1 - core), :], sib.at[i, :, packed(0, at_pair), :],
            fsib_s.at[i - near, at_pair], fsib_r.at[i - near, at_pair], sibling,
        )

    def red_rows(region, at_chip):
        return pl.ds(pl.multiple_of(region * (HALF // 2) + at_chip * tok, tok), tok)

    def back_copy(i, to):
        return remote(
            red.at[i, :, red_rows(1, to), :], rb_own.at[i, chip],
            back_s.at[i, to], back_r.at[i, chip], device(plane, to),
        )

    def back_arrival(i, source):
        return remote(
            red.at[i, :, red_rows(1, source), :], rb_own.at[i, source],
            back_s.at[i, source], back_r.at[i, source], device(plane, source),
        )

    def far_back_copy(i, to):
        return remote(
            red.at[i, :, red_rows(0, to), :], rb_far.at[i - near, chip],
            fback_s.at[i - near, to], fback_r.at[i - near, chip], device(prv, to),
        )

    def far_back_arrival(i, source):
        return remote(
            red.at[i, :, red_rows(0, source), :], rb_far.at[i, source],
            fback_s.at[i, source], fback_r.at[i, source], device(nxt, source),
        )

    pl.semaphore_wait(barrier, 3 * chips)

    @pl.loop(0, heads)
    def _(i):
        for k in range(1, chips):
            own_copy(i, (chip + k) % chips).start()

    @pl.loop(0, near)
    def _(i):
        for k in range(chips):
            far_copy(i, (chip + k) % chips).start()

    def start_forwards(i):
        for k in range(1, chips):
            own_arrival(i, (chip + k) % chips).wait_recv()
        for at_pair in range(pairs):
            forward(i, at_pair, core).start()

        @pl.when(i >= near)
        def _():
            for k in range(chips):
                far_arrival(i, (chip + k) % chips).wait_recv()
            for at_pair in range(pairs):
                far_forward(i, at_pair, core).start()

    def pass_on(i):
        for at_pair in range(pairs):
            sib_copy(i, at_pair).wait_recv()
            for w in range(2):
                red[i, w, packed(1, at_pair), :] = (
                    part[i, w, strip(HALF, at_pair, core), :].astype(jnp.float32)
                    + sib[i, w, packed(1, at_pair), :].astype(jnp.float32)
                ).astype(jnp.bfloat16)
        for k in range(1, chips):
            back_copy(i, (chip + k) % chips).start()

        @pl.when(i >= near)
        def _():
            for at_pair in range(pairs):
                far_sib_copy(i, at_pair).wait_recv()
                for w in range(2):
                    red[i, w, packed(0, at_pair), :] = (
                        part[i, w, strip(0, at_pair, core), :].astype(jnp.float32)
                        + sib[i, w, packed(0, at_pair), :].astype(jnp.float32)
                    ).astype(jnp.bfloat16)
            for k in range(chips):
                far_back_copy(i, (chip + k) % chips).start()

    start_forwards(0)
    ahead = lax.broadcasted_iota(jnp.int32, (CHUNK, nq), 0) - HALF - pos * tok
    ahead = ahead - lax.broadcasted_iota(jnp.int32, (CHUNK, nq), 1) % tok
    n_chunks = GROUP // CHUNK

    @pl.loop(0, heads)
    def _(i):
        head = perm[i]
        q = q_ref[head]
        d = d_ref[head]
        q_tr = q.T
        d_tr = d.T
        first = jnp.where(i < near, HALF // CHUNK, 0)
        for at_pair in range(pairs):
            forward(i, at_pair, 1 - core).wait_recv()

        @pl.when(i >= near)
        def _():
            for at_pair in range(pairs):
                far_forward(i, at_pair, 1 - core).wait_recv()

        def score_step(c, top):
            at = pl.ds(pl.multiple_of(c * CHUNK, CHUNK), CHUNK)
            s = nt(kv[i, 0, at, :], q_tr)
            s = jnp.where(ahead <= -c * CHUNK, s, MASKED)
            scores[at, :] = s
            return jnp.maximum(top, jnp.max(s.reshape(CHUNK // 8, 8, nq), axis=0))

        top = lax.fori_loop(first, n_chunks, score_step, jnp.full((8, nq), MASKED, jnp.float32))
        top = jnp.max(top, axis=0, keepdims=True)
        o_tr[...] = jnp.zeros_like(o_tr)

        def prob_step(c, total):
            at = pl.ds(pl.multiple_of(c * CHUNK, CHUNK), CHUNK)
            p = jnp.exp2((scores[at, :] - top) * to_exp2)
            scores[at, :] = p
            o_tr[...] += tn(kv[i, 1, at, :], p.astype(jnp.bfloat16))
            return total + jnp.sum(p.reshape(CHUNK // 8, 8, nq), axis=0)

        total = lax.fori_loop(first, n_chunks, prob_step, jnp.zeros((8, nq), jnp.float32))
        inverse = 1.0 / jnp.sum(total, axis=0, keepdims=True)
        attended = (o_tr[...] * inverse).astype(jnp.bfloat16)
        o_buf[i] = attended.T
        row_dot = jnp.sum(attended.astype(jnp.float32) * d_tr.astype(jnp.float32), axis=0, keepdims=True)
        dq_tr[...] = jnp.zeros_like(dq_tr)

        @pl.when(i < heads - 1)
        def _():
            start_forwards(i + 1)

        @pl.loop(first, n_chunks)
        def _(c):
            at = pl.ds(pl.multiple_of(c * CHUNK, CHUNK), CHUNK)
            k_part = kv[i, 0, at, :]
            p = scores[at, :] * inverse
            ds = (p * (nt(kv[i, 1, at, :], d_tr) - row_dot)).astype(jnp.bfloat16)
            part[i, 1, at, :] = nt(p.astype(jnp.bfloat16), d).astype(jnp.bfloat16)
            part[i, 0, at, :] = (nt(ds, q) * scaling).astype(jnp.bfloat16)
            dq_tr[...] += tn(k_part, ds)

        dq_buf[i] = (dq_tr[...] * scaling).astype(jnp.bfloat16).T
        for at_pair in range(pairs):
            sib_copy(i, at_pair).start()

        @pl.when(i >= near)
        def _():
            for at_pair in range(pairs):
                far_sib_copy(i, at_pair).start()

        @pl.when(i > 0)
        def _():
            pass_on(i - 1)

    pass_on(heads - 1)
    for h in range(heads):
        o_ref[h] = o_buf[inv[h]]
        dq_ref[h] = dq_buf[inv[h]]

    @pl.loop(0, heads)
    def _(i):
        for w in range(2):
            fin[i, w] = red[i, w, red_rows(1, chip), :].astype(jnp.float32)
        for k in range(1, chips):
            source = (chip + k) % chips
            back_arrival(i, source).wait_recv()
            for w in range(2):
                fin[i, w] += rb_own[i, source, w].astype(jnp.float32)

        @pl.when(i < near)
        def _():
            for k in range(chips):
                source = (chip + k) % chips
                far_back_arrival(i, source).wait_recv()
                for w in range(2):
                    fin[i, w] += rb_far[i, source, w].astype(jnp.float32)

    for h in range(heads):
        dk_ref[h] = fin[inv[h], 0].astype(jnp.bfloat16)
        dv_ref[h] = fin[inv[h], 1].astype(jnp.bfloat16)

    @pl.loop(0, heads)
    def _(i):
        for k in range(1, chips):
            to = (chip + k) % chips
            own_copy(i, to).wait_send()
            back_copy(i, to).wait_send()
        for at_pair in range(pairs):
            forward(i, at_pair, core).wait_send()
            sib_copy(i, at_pair).wait_send()

        @pl.when(i < near)
        def _():
            for k in range(chips):
                far_copy(i, (chip + k) % chips).wait_send()

        @pl.when(i >= near)
        def _():
            for k in range(chips):
                far_back_copy(i, (chip + k) % chips).wait_send()
            for at_pair in range(pairs):
                far_forward(i, at_pair, core).wait_send()
                far_sib_copy(i, at_pair).wait_send()


def local(n_seq, n_head, queries, keys, values, d_attended, shift_amounts):
    tok, heads, per, hd = queries.shape
    near = heads // 2
    nq = per * tok
    pairs = HALF // (tok * n_head) // 2
    chips = pairs * n_head

    def rows_first(a):
        return jnp.transpose(a, (1, 2, 0, 3)).reshape(heads, nq, hd)

    def tokens_first(a):
        return jnp.transpose(a.reshape(heads, per, tok, hd), (2, 0, 1, 3))

    vmem = pl.BlockSpec(memory_space=pltpu.VMEM)
    bf16, f32 = jnp.bfloat16, jnp.float32
    dma = pltpu.SemaphoreType.DMA
    wide = jax.ShapeDtypeStruct((heads, nq, hd), bf16)
    thin = jax.ShapeDtypeStruct((heads, tok, hd), bf16)
    o, dq, dk, dv = pl.pallas_call(
        functools.partial(kernel, n_seq, n_head, tok),
        out_shape=(wide, wide, thin, thin),
        in_specs=[pl.BlockSpec(memory_space=pltpu.SMEM)] + [vmem] * 4,
        out_specs=(vmem,) * 4,
        scratch_shapes=[
            pltpu.VMEM((heads, 2, GROUP, hd), bf16),
            pltpu.VMEM((heads, 2, GROUP, hd), bf16),
            pltpu.VMEM((heads, 2, HALF, hd), bf16),
            pltpu.VMEM((heads, 2, HALF, hd), bf16),
            pltpu.VMEM((heads, chips, 2, tok, hd), bf16),
            pltpu.VMEM((near, chips, 2, tok, hd), bf16),
            pltpu.VMEM((GROUP, nq), f32),
            pltpu.VMEM((hd, nq), f32),
            pltpu.VMEM((hd, nq), f32),
            pltpu.VMEM((heads, nq, hd), bf16),
            pltpu.VMEM((heads, nq, hd), bf16),
            pltpu.VMEM((heads, 2, tok, hd), f32),
            pltpu.SMEM((heads,), jnp.int32),
            pltpu.SMEM((heads,), jnp.int32),
            dma((heads, chips)), dma((heads, chips)), dma((near, chips)), dma((near, chips)),
            dma((heads, pairs)), dma((heads, pairs)), dma((near, pairs)), dma((near, pairs)),
            dma((heads, pairs)), dma((heads, pairs)), dma((near, pairs)), dma((near, pairs)),
            dma((heads, chips)), dma((heads, chips)), dma((near, chips)), dma((near, chips)),
        ],
        compiler_params=pltpu.CompilerParams(
            collective_id=0, has_side_effects=True, vmem_limit_bytes=56 * 1024 * 1024
        ),
    )(
        shift_amounts,
        rows_first(queries),
        jnp.transpose(keys, (1, 0, 2)),
        jnp.transpose(values, (1, 0, 2)),
        rows_first(d_attended),
    )
    return (
        tokens_first(o),
        tokens_first(dq),
        jnp.transpose(dk, (1, 0, 2)),
        jnp.transpose(dv, (1, 0, 2)),
    )


def solution(mesh):
    wide = P(("seq", "head"), None, None, None)
    thin = P(("seq", "head"), None, None)
    return jax.shard_map(
        functools.partial(local, mesh.shape["seq"], mesh.shape["head"]),
        mesh=mesh,
        in_specs=(wide, thin, thin, wide, P()),
        out_specs=(wide, wide, thin, thin),
        check_vma=False,
    )
```

profile of v0, /device:TPU:0, one launch (start us, length us, event | category | flops | bytes accessed | tf_op | source)
XLA Modules:
  0.0 99.0 jit_solution(15665542446179270302)
XLA Ops:
  0.6 0.0 copy-start
  0.6 2.0 %copy_bitcast_fusion.2 = (bf16[8,128,128]{2,1,0:T(8,128)(2,1)}, bf16[8,128,128]{2,1,0:T(8,128)(2,1)}) fusion(bf16[128,8,128]{2,1,0:T(8,128)(2,1)} %param.7, bf16[128,8,128]{2,1,0:T(8,128)(2,1)} %param.6), kind=kLoop, calls=%fused_computation.2 | loop fusion | bytes 1048576 | tf_op jit(solution)/shard_map/transpose | solution.py:389
  2.6 0.0 copy-done
  2.6 0.0 copy-start.1
  2.6 1.4 %copy.9 = bf16[8,4,128,128]{3,2,1,0:T(8,128)(2,1)} copy(bf16[8,4,128,128]{3,1,0,2:T(4,128)(2,1)S(1)} %bitcast.20) | data formatting | bytes 2097152 | tf_op jit(solution)/shard_map/transpose | solution.py:347
  4.0 0.0 copy-done.1
  4.0 1.4 %copy.12 = bf16[8,4,128,128]{3,2,1,0:T(8,128)(2,1)} copy(bf16[8,4,128,128]{3,1,0,2:T(4,128)(2,1)S(1)} %bitcast.21) | data formatting | bytes 2097152 | tf_op jit(solution)/shard_map/transpose | solution.py:347
  5.4 86.8 %shard_map.84 = (bf16[8,512,128]{2,1,0:T(8,128)(2,1)}, bf16[8,512,128]{2,1,0:T(8,128)(2,1)}, bf16[8,128,128]{2,1,0:T(8,128)(2,1)}, bf16[8,128,128]{2,1,0:T(8,128)(2,1)}) custom-call(s32[8]{0:T(128)} %shift_ref.1, bf16[8,512,128]{2,1,0:T(8,128)(2,1)} %bitcast.18, bf16[8,128,128]{2,1,0:T(8,128)(2,1)} %get-tuple-element.17.k_ref, ...), custom_call_target="tpu_custom_call" | custom-call | tf_op jit(solution)/shard_map/pallas_call | solution.py:357
  92.3 0.0 copy-start.2
  92.3 3.1 %copy.22 = bf16[8,4,128,128]{3,1,0,2:T(4,128)(2,1)} copy(bf16[8,4,128,128]{3,2,1,0:T(8,128)(2,1)} %bitcast.25) | data formatting | bytes 2097152 | tf_op jit(solution)/shard_map/reshape | solution.py:350
  95.4 0.0 copy-done.2
  95.4 0.0 copy-start.4
  95.4 1.8 %copy.21 = bf16[8,4,128,128]{3,1,0,2:T(4,128)(2,1)} copy(bf16[8,4,128,128]{3,2,1,0:T(8,128)(2,1)S(1)} %bitcast.24) | data formatting | bytes 2097152 | tf_op jit(solution)/shard_map/reshape | solution.py:350
  97.2 0.0 copy-done.4
  97.2 0.0 copy-start.3
  97.2 0.9 copy.15
  98.0 0.1 copy-done.3
  98.1 0.9 copy.16
Async XLA Ops:
  0.6 2.0 %copy-start = (bf16[128,8,4,128]{3,2,1,0:T(4,128)(2,1)S(1)}, bf16[128,8,4,128]{3,2,1,0:T(4,128)(2,1)}, u32[]{:S(2)}) copy-start(bf16[128,8,4,128]{3,2,1,0:T(4,128)(2,1)} %param.5) | copy-start | bytes 3145732
  2.6 1.4 %copy-start.1 = (bf16[128,8,4,128]{3,2,1,0:T(4,128)(2,1)S(1)}, bf16[128,8,4,128]{3,2,1,0:T(4,128)(2,1)}, u32[]{:S(2)}) copy-start(bf16[128,8,4,128]{3,2,1,0:T(4,128)(2,1)} %param.8) | copy-start | bytes 3145732
  92.3 3.1 %copy-start.2 = (bf16[8,512,128]{2,1,0:T(8,128)(2,1)S(1)}, bf16[8,512,128]{2,1,0:T(8,128)(2,1)}, u32[]{:S(2)}) copy-start(bf16[8,512,128]{2,1,0:T(8,128)(2,1)} %get-tuple-element.9) | copy-start | bytes 3145732
  95.4 1.8 %copy-start.4 = (bf16[8,128,128]{2,1,0:T(8,128)(2,1)S(1)}, bf16[8,128,128]{2,1,0:T(8,128)(2,1)}, u32[]{:S(2)}) copy-start(bf16[8,128,128]{2,1,0:T(8,128)(2,1)} %get-tuple-element.10) | copy-start | bytes 786436
  97.2 1.0 copy-start.3
where the time goes:
time: 99.2 us; the launch traced here: 99 us
  Pallas kernels  86.8 us (88%)
  local copies, waits for them, and re-layouts  11.5 us (12%)
    pallas_call x1, Pallas kernels, local(): pl.pallas_call(functools.partial(kernel, n_seq, n_head, tok), out_shape=(...  86.8 us
    reshape x2, local copies, waits for them, and re-layouts, tokens_first(): return jnp.transpose(a.reshape(heads, per, tok, hd), (2, 0, 1, 3))  4.87 us
    transpose x2, local copies, waits for them, and re-layouts, rows_first(): return jnp.transpose(a, (1, 2, 0, 3)).reshape(heads, nq, hd)  2.76 us
    transpose x1, local copies, waits for them, and re-layouts, local(): jnp.transpose(values, (1, 0, 2))  2 us

commit v1 on v0

--- a/solution.py
+++ b/solution.py
@@ -10,7 +10,7 @@
 
 GROUP = 2048
 HALF = GROUP // 2
-CHUNK = 256
+CHUNK = 512
 MASKED = -1e30
 MESH = pl.DeviceIdType.MESH
 
@@ -27,13 +27,14 @@
     n_seq, n_head, tok,
     shift_ref, q_ref, k_ref, v_ref, d_ref,
     o_ref, dq_ref, dk_ref, dv_ref,
-    kv, part, sib, red, rb_own, rb_far, scores, o_tr, dq_tr, o_buf, dq_buf, fin, perm, inv,
+    kv, part, sib, red, rb_own, rb_far, scores, o_tr, dq_tr, o_buf, dq_buf, fin, k_by, v_by, perm, inv,
     own_s, own_r, far_s, far_r, fwd_s, fwd_r, ffwd_s, ffwd_r,
     sib_s, sib_r, fsib_s, fsib_r, back_s, back_r, fback_s, fback_r,
 ):
-    heads = k_ref.shape[0]
+    heads = k_ref.shape[1]
     near = heads // 2
-    nq = q_ref.shape[1]
+    per = q_ref.shape[2]
+    nq = per * tok
     span = HALF // (tok * n_head)
     rows = tok * n_head
     pairs = span // 2
@@ -49,7 +50,8 @@
     pos = s_in * n_head + x
     nxt = (plane + 1) % n_planes
     prv = (plane + n_planes - 1) % n_planes
-    scaling = 1.0 / math.sqrt(k_ref.shape[2])
+    hd = k_ref.shape[2]
+    scaling = 1.0 / math.sqrt(hd)
     to_exp2 = scaling * math.log2(math.e)
 
     def device(at_plane, at_chip):
@@ -82,10 +84,12 @@
         inv[h] = ranks[h]
         perm[h] = sum(jnp.where(ranks[j] == h, j, 0) for j in range(heads))
 
+    k_by[...] = jnp.swapaxes(k_ref[...].astype(jnp.float32), 0, 1).astype(jnp.bfloat16)
+    v_by[...] = jnp.swapaxes(v_ref[...].astype(jnp.float32), 0, 1).astype(jnp.bfloat16)
     mine = pl.ds(pl.multiple_of(HALF + pos * tok, tok), tok)
     for i in range(heads):
-        kv[i, 0, mine, :] = k_ref[perm[i]]
-        kv[i, 1, mine, :] = v_ref[perm[i]]
+        kv[i, 0, mine, :] = k_by[perm[i]]
+        kv[i, 1, mine, :] = v_by[perm[i]]
 
     def remote(src, dst, ssem, rsem, dev):
         return pltpu.make_async_remote_copy(
@@ -169,7 +173,11 @@
     @pl.loop(0, heads)
     def _(i):
         for k in range(1, chips):
-            own_copy(i, (chip + k) % chips).start()
+            to = (chip + k) % chips
+
+            @pl.when(to // n_head >= y)
+            def _():
+                own_copy(i, to).start()
 
     @pl.loop(0, near)
     def _(i):
@@ -178,9 +186,17 @@
 
     def start_forwards(i):
         for k in range(1, chips):
-            own_arrival(i, (chip + k) % chips).wait_recv()
+            source = (chip + k) % chips
+
+            @pl.when(source // n_head <= y)
+            def _():
+                own_arrival(i, source).wait_recv()
+
         for at_pair in range(pairs):
-            forward(i, at_pair, core).start()
+
+            @pl.when(at_pair <= y)
+            def _():
+                forward(i, at_pair, core).start()
 
         @pl.when(i >= near)
         def _():
@@ -191,14 +207,22 @@
 
     def pass_on(i):
         for at_pair in range(pairs):
-            sib_copy(i, at_pair).wait_recv()
-            for w in range(2):
-                red[i, w, packed(1, at_pair), :] = (
-                    part[i, w, strip(HALF, at_pair, core), :].astype(jnp.float32)
-                    + sib[i, w, packed(1, at_pair), :].astype(jnp.float32)
-                ).astype(jnp.bfloat16)
+
+            @pl.when(at_pair <= y)
+            def _():
+                sib_copy(i, at_pair).wait_recv()
+                for w in range(2):
+                    red[i, w, packed(1, at_pair), :] = (
+                        part[i, w, strip(HALF, at_pair, core), :].astype(jnp.float32)
+                        + sib[i, w, packed(1, at_pair), :].astype(jnp.float32)
+                    ).astype(jnp.bfloat16)
+
         for k in range(1, chips):
-            back_copy(i, (chip + k) % chips).start()
+            to = (chip + k) % chips
+
+            @pl.when(to // n_head <= y)
+            def _():
+                back_copy(i, to).start()
 
         @pl.when(i >= near)
         def _():
@@ -214,19 +238,22 @@
 
     start_forwards(0)
     ahead = lax.broadcasted_iota(jnp.int32, (CHUNK, nq), 0) - HALF - pos * tok
-    ahead = ahead - lax.broadcasted_iota(jnp.int32, (CHUNK, nq), 1) % tok
-    n_chunks = GROUP // CHUNK
+    ahead = ahead - lax.broadcasted_iota(jnp.int32, (CHUNK, nq), 1) // per
+    n_chunks = (HALF + (y + 1) * 2 * rows) // CHUNK
 
     @pl.loop(0, heads)
     def _(i):
         head = perm[i]
-        q = q_ref[head]
-        d = d_ref[head]
+        q = q_ref[:, head].reshape(nq, hd)
+        d = d_ref[:, head].reshape(nq, hd)
         q_tr = q.T
         d_tr = d.T
         first = jnp.where(i < near, HALF // CHUNK, 0)
         for at_pair in range(pairs):
-            forward(i, at_pair, 1 - core).wait_recv()
+
+            @pl.when(at_pair <= y)
+            def _():
+                forward(i, at_pair, 1 - core).wait_recv()
 
         @pl.when(i >= near)
         def _():
@@ -274,7 +301,10 @@
 
         dq_buf[i] = (dq_tr[...] * scaling).astype(jnp.bfloat16).T
         for at_pair in range(pairs):
-            sib_copy(i, at_pair).start()
+
+            @pl.when(at_pair <= y)
+            def _():
+                sib_copy(i, at_pair).start()
 
         @pl.when(i >= near)
         def _():
@@ -287,8 +317,8 @@
 
     pass_on(heads - 1)
     for h in range(heads):
-        o_ref[h] = o_buf[inv[h]]
-        dq_ref[h] = dq_buf[inv[h]]
+        o_ref[:, h] = o_buf[inv[h]].reshape(tok, per, hd)
+        dq_ref[:, h] = dq_buf[inv[h]].reshape(tok, per, hd)
 
     @pl.loop(0, heads)
     def _(i):
@@ -296,9 +326,12 @@
             fin[i, w] = red[i, w, red_rows(1, chip), :].astype(jnp.float32)
         for k in range(1, chips):
             source = (chip + k) % chips
-            back_arrival(i, source).wait_recv()
-            for w in range(2):
-                fin[i, w] += rb_own[i, source, w].astype(jnp.float32)
+
+            @pl.when(source // n_head >= y)
+            def _():
+                back_arrival(i, source).wait_recv()
+                for w in range(2):
+                    fin[i, w] += rb_own[i, source, w].astype(jnp.float32)
 
         @pl.when(i < near)
         def _():
@@ -308,19 +341,28 @@
                 for w in range(2):
                     fin[i, w] += rb_far[i, source, w].astype(jnp.float32)
 
-    for h in range(heads):
-        dk_ref[h] = fin[inv[h], 0].astype(jnp.bfloat16)
-        dv_ref[h] = fin[inv[h], 1].astype(jnp.bfloat16)
+    dk_ref[...] = jnp.swapaxes(jnp.stack([fin[inv[h], 0] for h in range(heads)]), 0, 1).astype(jnp.bfloat16)
+    dv_ref[...] = jnp.swapaxes(jnp.stack([fin[inv[h], 1] for h in range(heads)]), 0, 1).astype(jnp.bfloat16)
 
     @pl.loop(0, heads)
     def _(i):
         for k in range(1, chips):
             to = (chip + k) % chips
-            own_copy(i, to).wait_send()
-            back_copy(i, to).wait_send()
+
+            @pl.when(to // n_head >= y)
+            def _():
+                own_copy(i, to).wait_send()
+
+            @pl.when(to // n_head <= y)
+            def _():
+                back_copy(i, to).wait_send()
+
         for at_pair in range(pairs):
-            forward(i, at_pair, core).wait_send()
-            sib_copy(i, at_pair).wait_send()
+
+            @pl.when(at_pair <= y)
+            def _():
+                forward(i, at_pair, core).wait_send()
+                sib_copy(i, at_pair).wait_send()
 
         @pl.when(i < near)
         def _():
@@ -343,17 +385,11 @@
     pairs = HALF // (tok * n_head) // 2
     chips = pairs * n_head
 
-    def rows_first(a):
-        return jnp.transpose(a, (1, 2, 0, 3)).reshape(heads, nq, hd)
-
-    def tokens_first(a):
-        return jnp.transpose(a.reshape(heads, per, tok, hd), (2, 0, 1, 3))
-
     vmem = pl.BlockSpec(memory_space=pltpu.VMEM)
     bf16, f32 = jnp.bfloat16, jnp.float32
     dma = pltpu.SemaphoreType.DMA
-    wide = jax.ShapeDtypeStruct((heads, nq, hd), bf16)
-    thin = jax.ShapeDtypeStruct((heads, tok, hd), bf16)
+    wide = jax.ShapeDtypeStruct((tok, heads, per, hd), bf16)
+    thin = jax.ShapeDtypeStruct((tok, heads, hd), bf16)
     o, dq, dk, dv = pl.pallas_call(
         functools.partial(kernel, n_seq, n_head, tok),
         out_shape=(wide, wide, thin, thin),
@@ -372,6 +408,8 @@
             pltpu.VMEM((heads, nq, hd), bf16),
             pltpu.VMEM((heads, nq, hd), bf16),
             pltpu.VMEM((heads, 2, tok, hd), f32),
+            pltpu.VMEM((heads, tok, hd), bf16),
+            pltpu.VMEM((heads, tok, hd), bf16),
             pltpu.SMEM((heads,), jnp.int32),
             pltpu.SMEM((heads,), jnp.int32),
             dma((heads, chips)), dma((heads, chips)), dma((near, chips)), dma((near, chips)),
@@ -382,19 +420,8 @@
         compiler_params=pltpu.CompilerParams(
             collective_id=0, has_side_effects=True, vmem_limit_bytes=56 * 1024 * 1024
         ),
-    )(
-        shift_amounts,
-        rows_first(queries),
-        jnp.transpose(keys, (1, 0, 2)),
-        jnp.transpose(values, (1, 0, 2)),
-        rows_first(d_attended),
-    )
-    return (
-        tokens_first(o),
-        tokens_first(dq),
-        jnp.transpose(dk, (1, 0, 2)),
-        jnp.transpose(dv, (1, 0, 2)),
-    )
+    )(shift_amounts, queries, keys, values, d_attended)
+    return o, dq, dk, dv
 
 
 def solution(mesh):

time: 99.2 us -> 85.7 us (0.86)
  Pallas kernels: 86.8 us -> 79.3 us
  local copies, waits for them, and re-layouts: 11.5 us -> 5.48 us
    pallas_call x1, Pallas kernels: 86.8 us -> 79.3 us  [local(): pl.pallas_call(functools.partial(kernel, n_seq, n_head, tok), out_shape=(...]
    reshape x2 -> x0, local copies, waits for them, and re-layouts: 4.87 us -> none  [tokens_first(): return jnp.transpose(a.reshape(heads, per, tok, hd), (2, 0, 1, 3))]
    transpose x3 -> x0, local copies, waits for them, and re-layouts: 4.76 us -> none  [the longest x2 2.76 us: rows_first(): return jnp.transpose(a, (1, 2, 0, 3)).reshape(heads, nq, hd)]
    unnamed x12 -> x10, local copies, waits for them, and re-layouts: 1.84 us -> 5.48 us
where the time goes in v1:
time: 85.7 us; the launch traced here: 85.4 us
  Pallas kernels  79.3 us (93%)
  local copies, waits for them, and re-layouts  5.48 us (6%)
    pallas_call x1, Pallas kernels, local(): pl.pallas_call(functools.partial(kernel, n_seq, n_head, tok), out_shape=(...  79.3 us
    unnamed x10, local copies, waits for them, and re-layouts  5.48 us

profile of v1, /device:TPU:0, one launch (start us, length us, event | category | flops | bytes accessed | tf_op | source)
XLA Modules:
  0.0 85.4 jit_solution(3961922806671891693)
XLA Ops:
  0.6 79.3 %shard_map.84 = (bf16[128,8,4,128]{3,2,1,0:T(4,128)(2,1)}, bf16[128,8,4,128]{3,2,1,0:T(4,128)(2,1)}, bf16[128,8,128]{2,1,0:T(8,128)(2,1)}, bf16[128,8,128]{2,1,0:T(8,128)(2,1)}) custom-call(s32[8]{0:T(128)} %shift_ref.1, bf16[128,8,4,128]{3,2,1,0:T(4,128)(2,1)} %q_ref.1, bf16[128,8,128]{2,1,0:T(8,128)(2,1)} %k_ref.1, bf16[128,8,128]{2,1,0:T(8,128)(2,1)} %v_ref.1, ...), custom_call_target="tpu_custom_call" | custom-call | tf_op jit(solution)/shard_map/pallas_call | solution.py:393
  79.9 0.0 copy-start
  79.9 2.6 %copy.13 = bf16[128,8,4,128]{3,2,1,0:T(4,128)(2,1)} copy(bf16[128,8,4,128]{3,2,1,0:T(4,128)(2,1)} %get-tuple-element.8) | data formatting | bytes 2097152
  82.6 0.0 copy-done
  82.6 0.0 copy-start.2
  82.6 1.0 %copy.14 = bf16[128,8,4,128]{3,2,1,0:T(4,128)(2,1)} copy(bf16[128,8,4,128]{3,2,1,0:T(4,128)(2,1)S(1)} %copy-done) | data formatting | bytes 2097152
  83.6 0.1 copy-done.2
  83.7 0.0 copy-start.1
  83.7 0.7 copy.15
  84.4 0.3 copy-done.1
  84.7 0.7 copy.16
Async XLA Ops:
  79.9 2.7 %copy-start = (bf16[128,8,4,128]{3,2,1,0:T(4,128)(2,1)S(1)}, bf16[128,8,4,128]{3,2,1,0:T(4,128)(2,1)}, u32[]{:S(2)}) copy-start(bf16[128,8,4,128]{3,2,1,0:T(4,128)(2,1)} %get-tuple-element.9) | copy-start | bytes 3145732
  82.6 1.1 %copy-start.2 = (bf16[128,8,128]{2,1,0:T(8,128)(2,1)S(1)}, bf16[128,8,128]{2,1,0:T(8,128)(2,1)}, u32[]{:S(2)}) copy-start(bf16[128,8,128]{2,1,0:T(8,128)(2,1)} %get-tuple-element.10) | copy-start | bytes 786436
  83.7 1.0 %copy-start.1 = (bf16[128,8,128]{2,1,0:T(8,128)(2,1)S(1)}, bf16[128,8,128]{2,1,0:T(8,128)(2,1)}, u32[]{:S(2)}) copy-start(bf16[128,8,128]{2,1,0:T(8,128)(2,1)} %get-tuple-element.11) | copy-start | bytes 786436

commit v2 on v1

--- a/solution.py
+++ b/solution.py
@@ -27,7 +27,7 @@
     n_seq, n_head, tok,
     shift_ref, q_ref, k_ref, v_ref, d_ref,
     o_ref, dq_ref, dk_ref, dv_ref,
-    kv, part, sib, red, rb_own, rb_far, scores, o_tr, dq_tr, o_buf, dq_buf, fin, k_by, v_by, perm, inv,
+    kv, part, sib, red, rb_own, rb_far, scores, o_tr, dq_tr, o_buf, dq_buf, fin, k_by, v_by, q_by, d_by, q_by_tr, d_by_tr, perm, inv,
     own_s, own_r, far_s, far_r, fwd_s, fwd_r, ffwd_s, ffwd_r,
     sib_s, sib_r, fsib_s, fsib_r, back_s, back_r, fback_s, fback_r,
 ):
@@ -170,8 +170,12 @@
 
     pl.semaphore_wait(barrier, 3 * chips)
 
+    def order(t):
+        return ((t + near - 2) % (heads - 1) + 1) * ((t + heads - 2) // (heads - 1))
+
     @pl.loop(0, heads)
-    def _(i):
+    def _(t):
+        i = order(t)
         for k in range(1, chips):
             to = (chip + k) % chips
 
@@ -179,10 +183,10 @@
             def _():
                 own_copy(i, to).start()
 
-    @pl.loop(0, near)
-    def _(i):
-        for k in range(chips):
-            far_copy(i, (chip + k) % chips).start()
+        @pl.when(i >= near)
+        def _():
+            for k in range(chips):
+                far_copy(i - near, (chip + k) % chips).start()
 
     def start_forwards(i):
         for k in range(1, chips):
@@ -236,18 +240,25 @@
             for k in range(chips):
                 far_back_copy(i, (chip + k) % chips).start()
 
+    def re_lay(i):
+        head = perm[i]
+        q = q_ref[:, head].reshape(nq, hd)
+        d = d_ref[:, head].reshape(nq, hd)
+        q_by[i] = q
+        d_by[i] = d
+        q_by_tr[i] = q.T
+        d_by_tr[i] = d.T
+
+    pl.loop(0, near)(re_lay)
     start_forwards(0)
+    pl.loop(near, heads)(re_lay)
     ahead = lax.broadcasted_iota(jnp.int32, (CHUNK, nq), 0) - HALF - pos * tok
     ahead = ahead - lax.broadcasted_iota(jnp.int32, (CHUNK, nq), 1) // per
     n_chunks = (HALF + (y + 1) * 2 * rows) // CHUNK
 
     @pl.loop(0, heads)
-    def _(i):
-        head = perm[i]
-        q = q_ref[:, head].reshape(nq, hd)
-        d = d_ref[:, head].reshape(nq, hd)
-        q_tr = q.T
-        d_tr = d.T
+    def _(t):
+        i = order(t)
         first = jnp.where(i < near, HALF // CHUNK, 0)
         for at_pair in range(pairs):
 
@@ -262,7 +273,7 @@
 
         def score_step(c, top):
             at = pl.ds(pl.multiple_of(c * CHUNK, CHUNK), CHUNK)
-            s = nt(kv[i, 0, at, :], q_tr)
+            s = nt(kv[i, 0, at, :], q_by_tr[i])
             s = jnp.where(ahead <= -c * CHUNK, s, MASKED)
             scores[at, :] = s
             return jnp.maximum(top, jnp.max(s.reshape(CHUNK // 8, 8, nq), axis=0))
@@ -270,6 +281,10 @@
         top = lax.fori_loop(first, n_chunks, score_step, jnp.full((8, nq), MASKED, jnp.float32))
         top = jnp.max(top, axis=0, keepdims=True)
         o_tr[...] = jnp.zeros_like(o_tr)
+
+        @pl.when(t > 0)
+        def _():
+            pass_on(order(t - 1))
 
         def prob_step(c, total):
             at = pl.ds(pl.multiple_of(c * CHUNK, CHUNK), CHUNK)
@@ -282,21 +297,21 @@
         inverse = 1.0 / jnp.sum(total, axis=0, keepdims=True)
         attended = (o_tr[...] * inverse).astype(jnp.bfloat16)
         o_buf[i] = attended.T
-        row_dot = jnp.sum(attended.astype(jnp.float32) * d_tr.astype(jnp.float32), axis=0, keepdims=True)
+        row_dot = jnp.sum(attended.astype(jnp.float32) * d_by_tr[i].astype(jnp.float32), axis=0, keepdims=True)
         dq_tr[...] = jnp.zeros_like(dq_tr)
 
-        @pl.when(i < heads - 1)
-        def _():
-            start_forwards(i + 1)
+        @pl.when(t < heads - 1)
+        def _():
+            start_forwards(order(t + 1))
 
         @pl.loop(first, n_chunks)
         def _(c):
             at = pl.ds(pl.multiple_of(c * CHUNK, CHUNK), CHUNK)
             k_part = kv[i, 0, at, :]
             p = scores[at, :] * inverse
-            ds = (p * (nt(kv[i, 1, at, :], d_tr) - row_dot)).astype(jnp.bfloat16)
-            part[i, 1, at, :] = nt(p.astype(jnp.bfloat16), d).astype(jnp.bfloat16)
-            part[i, 0, at, :] = (nt(ds, q) * scaling).astype(jnp.bfloat16)
+            ds = (p * (nt(kv[i, 1, at, :], d_by_tr[i]) - row_dot)).astype(jnp.bfloat16)
+            part[i, 1, at, :] = nt(p.astype(jnp.bfloat16), d_by[i]).astype(jnp.bfloat16)
+            part[i, 0, at, :] = (nt(ds, q_by[i]) * scaling).astype(jnp.bfloat16)
             dq_tr[...] += tn(k_part, ds)
 
         dq_buf[i] = (dq_tr[...] * scaling).astype(jnp.bfloat16).T
@@ -311,11 +326,7 @@
             for at_pair in range(pairs):
                 far_sib_copy(i, at_pair).start()
 
-        @pl.when(i > 0)
-        def _():
-            pass_on(i - 1)
-
-    pass_on(heads - 1)
+    pass_on(near - 1)
     for h in range(heads):
         o_ref[:, h] = o_buf[inv[h]].reshape(tok, per, hd)
         dq_ref[:, h] = dq_buf[inv[h]].reshape(tok, per, hd)
@@ -378,6 +389,20 @@
                 far_sib_copy(i, at_pair).wait_send()
 
 
+def settle(parts, *refs):
+    sems = refs[-1]
+    copies = []
+    for j in range(4):
+        size = refs[j].shape[0] // parts
+        for part in range(parts):
+            at = pl.ds(part * size, size)
+            copies.append(pltpu.make_async_copy(refs[j].at[at], refs[j + 4].at[at], sems.at[j, part]))
+    for copy in copies:
+        copy.start()
+    for copy in copies:
+        copy.wait()
+
+
 def local(n_seq, n_head, queries, keys, values, d_attended, shift_amounts):
     tok, heads, per, hd = queries.shape
     near = heads // 2
@@ -390,7 +415,7 @@
     dma = pltpu.SemaphoreType.DMA
     wide = jax.ShapeDtypeStruct((tok, heads, per, hd), bf16)
     thin = jax.ShapeDtypeStruct((tok, heads, hd), bf16)
-    o, dq, dk, dv = pl.pallas_call(
+    results = pl.pallas_call(
         functools.partial(kernel, n_seq, n_head, tok),
         out_shape=(wide, wide, thin, thin),
         in_specs=[pl.BlockSpec(memory_space=pltpu.SMEM)] + [vmem] * 4,
@@ -410,6 +435,10 @@
             pltpu.VMEM((heads, 2, tok, hd), f32),
             pltpu.VMEM((heads, tok, hd), bf16),
             pltpu.VMEM((heads, tok, hd), bf16),
+            pltpu.VMEM((heads, nq, hd), bf16),
+            pltpu.VMEM((heads, nq, hd), bf16),
+            pltpu.VMEM((heads, hd, nq), bf16),
+            pltpu.VMEM((heads, hd, nq), bf16),
             pltpu.SMEM((heads,), jnp.int32),
             pltpu.SMEM((heads,), jnp.int32),
             dma((heads, chips)), dma((heads, chips)), dma((near, chips)), dma((near, chips)),
@@ -421,7 +450,15 @@
             collective_id=0, has_side_effects=True, vmem_limit_bytes=56 * 1024 * 1024
         ),
     )(shift_amounts, queries, keys, values, d_attended)
-    return o, dq, dk, dv
+    parts = 4
+    return pl.pallas_call(
+        functools.partial(settle, parts),
+        out_shape=(wide, wide, thin, thin),
+        in_specs=[pl.BlockSpec(memory_space=pl.ANY)] * 4,
+        out_specs=(pl.BlockSpec(memory_space=pl.ANY),) * 4,
+        scratch_shapes=[dma((4, parts))],
+        compiler_params=pltpu.CompilerParams(vmem_limit_bytes=60 * 1024 * 1024),
+    )(*results)
 
 
 def solution(mesh):

time: 85.7 us -> 153 us (1.79)
  Pallas kernels: 79.3 us -> 152 us
  local copies, waits for them, and re-layouts: 5.48 us -> 0 us
    pallas_call x0 -> x1, Pallas kernels: none -> 80.7 us  [local(): pl.pallas_call(functools.partial(settle, parts), out_shape=(wide, wide, t...]
    pallas_call x1, Pallas kernels: 79.3 us -> 71.4 us  [local(): pl.pallas_call(functools.partial(kernel, n_seq, n_head, tok), out_shape=(...]
    unnamed x10 -> x0, local copies, waits for them, and re-layouts: 5.48 us -> none
where the time goes in v2:
time: 153 us
  Pallas kernels  152 us (99%)
    pallas_call x1, Pallas kernels, local(): pl.pallas_call(functools.partial(settle, parts), out_shape=(wide, wide, t...  80.7 us
    pallas_call x1, Pallas kernels, local(): pl.pallas_call(functools.partial(kernel, n_seq, n_head, tok), out_shape=(...  71.4 us

profile of v2, /device:TPU:0, one launch (start us, length us, event | category | flops | bytes accessed | tf_op | source)
XLA Modules:
  0.0 152.7 jit_solution(17439604305661858417)
XLA Ops:
  0.6 71.4 %shard_map.84 = (bf16[128,8,4,128]{3,2,1,0:T(4,128)(2,1)}, bf16[128,8,4,128]{3,2,1,0:T(4,128)(2,1)}, bf16[128,8,128]{2,1,0:T(8,128)(2,1)}, bf16[128,8,128]{2,1,0:T(8,128)(2,1)}) custom-call(s32[8]{0:T(128)} %shift_ref.1, bf16[128,8,4,128]{3,2,1,0:T(4,128)(2,1)} %q_ref.1, bf16[128,8,128]{2,1,0:T(8,128)(2,1)} %k_ref.1, bf16[128,8,128]{2,1,0:T(8,128)(2,1)} %v_ref.1, ...), custom_call_target="tpu_custom_call" | custom-call | tf_op jit(solution)/shard_map/pallas_call | solution.py:418
  72.1 80.7 %shard_map.85 = (bf16[128,8,4,128]{3,2,1,0:T(4,128)(2,1)}, bf16[128,8,4,128]{3,2,1,0:T(4,128)(2,1)}, bf16[128,8,128]{2,1,0:T(8,128)(2,1)}, bf16[128,8,128]{2,1,0:T(8,128)(2,1)}) custom-call(bf16[128,8,4,128]{3,2,1,0:T(4,128)(2,1)} %get-tuple-element.8.refs_0_, bf16[128,8,4,128]{3,2,1,0:T(4,128)(2,1)} %get-tuple-element.9.refs_1_, ...), custom_call_target="tpu_custom_call" | custom-call | tf_op jit(solution)/shard_map/pallas_call | solution.py:454

commit v3 on v2

--- a/solution.py
+++ b/solution.py
@@ -10,7 +10,6 @@
 
 GROUP = 2048
 HALF = GROUP // 2
-CHUNK = 512
 MASKED = -1e30
 MESH = pl.DeviceIdType.MESH
 
@@ -27,7 +26,7 @@
     n_seq, n_head, tok,
     shift_ref, q_ref, k_ref, v_ref, d_ref,
     o_ref, dq_ref, dk_ref, dv_ref,
-    kv, part, sib, red, rb_own, rb_far, scores, o_tr, dq_tr, o_buf, dq_buf, fin, k_by, v_by, q_by, d_by, q_by_tr, d_by_tr, perm, inv,
+    kv, part, sib, red, rb_own, rb_far, scores, top8, total8, o_tr, dq_tr, o_buf, dq_buf, fin, k_by, v_by, q_by, d_by, q_by_tr, d_by_tr, perm, inv,
     own_s, own_r, far_s, far_r, fwd_s, fwd_r, ffwd_s, ffwd_r,
     sib_s, sib_r, fsib_s, fsib_r, back_s, back_r, fback_s, fback_r,
 ):
@@ -252,14 +251,22 @@
     pl.loop(0, near)(re_lay)
     start_forwards(0)
     pl.loop(near, heads)(re_lay)
-    ahead = lax.broadcasted_iota(jnp.int32, (CHUNK, nq), 0) - HALF - pos * tok
-    ahead = ahead - lax.broadcasted_iota(jnp.int32, (CHUNK, nq), 1) // per
-    n_chunks = (HALF + (y + 1) * 2 * rows) // CHUNK
+    short = 2 * rows
+
+    def blocks(i, step):
+        @pl.when(i >= near)
+        def _():
+            step(0, HALF)
+
+        for last in range(pairs):
+
+            @pl.when(y == last)
+            def _():
+                step(HALF, (last + 1) * short)
 
     @pl.loop(0, heads)
     def _(t):
         i = order(t)
-        first = jnp.where(i < near, HALF // CHUNK, 0)
         for at_pair in range(pairs):
 
             @pl.when(at_pair <= y)
@@ -271,30 +278,36 @@
             for at_pair in range(pairs):
                 far_forward(i, at_pair, 1 - core).wait_recv()
 
-        def score_step(c, top):
-            at = pl.ds(pl.multiple_of(c * CHUNK, CHUNK), CHUNK)
+        top8[...] = jnp.full_like(top8, MASKED)
+        total8[...] = jnp.zeros_like(total8)
+
+        def score_step(start, size):
+            at = pl.ds(start, size)
             s = nt(kv[i, 0, at, :], q_by_tr[i])
-            s = jnp.where(ahead <= -c * CHUNK, s, MASKED)
+            if start == HALF:
+                key_at = lax.broadcasted_iota(jnp.int32, (size, nq), 0)
+                query_at = lax.broadcasted_iota(jnp.int32, (1, nq), 1) // per + pos * tok
+                s = jnp.where(key_at <= query_at, s, MASKED)
             scores[at, :] = s
-            return jnp.maximum(top, jnp.max(s.reshape(CHUNK // 8, 8, nq), axis=0))
-
-        top = lax.fori_loop(first, n_chunks, score_step, jnp.full((8, nq), MASKED, jnp.float32))
-        top = jnp.max(top, axis=0, keepdims=True)
+            top8[...] = jnp.maximum(top8[...], jnp.max(s.reshape(size // 8, 8, nq), axis=0))
+
+        blocks(i, score_step)
+        top = jnp.max(top8[...], axis=0, keepdims=True)
         o_tr[...] = jnp.zeros_like(o_tr)
 
         @pl.when(t > 0)
         def _():
             pass_on(order(t - 1))
 
-        def prob_step(c, total):
-            at = pl.ds(pl.multiple_of(c * CHUNK, CHUNK), CHUNK)
+        def prob_step(start, size):
+            at = pl.ds(start, size)
             p = jnp.exp2((scores[at, :] - top) * to_exp2)
             scores[at, :] = p
             o_tr[...] += tn(kv[i, 1, at, :], p.astype(jnp.bfloat16))
-            return total + jnp.sum(p.reshape(CHUNK // 8, 8, nq), axis=0)
-
-        total = lax.fori_loop(first, n_chunks, prob_step, jnp.zeros((8, nq), jnp.float32))
-        inverse = 1.0 / jnp.sum(total, axis=0, keepdims=True)
+            total8[...] += jnp.sum(p.reshape(size // 8, 8, nq), axis=0)
+
+        blocks(i, prob_step)
+        inverse = 1.0 / jnp.sum(total8[...], axis=0, keepdims=True)
         attended = (o_tr[...] * inverse).astype(jnp.bfloat16)
         o_buf[i] = attended.T
         row_dot = jnp.sum(attended.astype(jnp.float32) * d_by_tr[i].astype(jnp.float32), axis=0, keepdims=True)
@@ -304,15 +317,16 @@
         def _():
             start_forwards(order(t + 1))
 
-        @pl.loop(first, n_chunks)
-        def _(c):
-            at = pl.ds(pl.multiple_of(c * CHUNK, CHUNK), CHUNK)
+        def grad_step(start, size):
+            at = pl.ds(start, size)
             k_part = kv[i, 0, at, :]
             p = scores[at, :] * inverse
             ds = (p * (nt(kv[i, 1, at, :], d_by_tr[i]) - row_dot)).astype(jnp.bfloat16)
             part[i, 1, at, :] = nt(p.astype(jnp.bfloat16), d_by[i]).astype(jnp.bfloat16)
             part[i, 0, at, :] = (nt(ds, q_by[i]) * scaling).astype(jnp.bfloat16)
             dq_tr[...] += tn(k_part, ds)
+
+        blocks(i, grad_step)
 
         dq_buf[i] = (dq_tr[...] * scaling).astype(jnp.bfloat16).T
         for at_pair in range(pairs):
@@ -428,6 +442,8 @@
             pltpu.VMEM((heads, chips, 2, tok, hd), bf16),
             pltpu.VMEM((near, chips, 2, tok, hd), bf16),
             pltpu.VMEM((GROUP, nq), f32),
+            pltpu.VMEM((8, nq), f32),
+            pltpu.VMEM((8, nq), f32),
             pltpu.VMEM((hd, nq), f32),
             pltpu.VMEM((hd, nq), f32),
             pltpu.VMEM((heads, nq, hd), bf16),
@@ -454,10 +470,9 @@
     return pl.pallas_call(
         functools.partial(settle, parts),
         out_shape=(wide, wide, thin, thin),
-        in_specs=[pl.BlockSpec(memory_space=pl.ANY)] * 4,
+        in_specs=[vmem] * 4,
         out_specs=(pl.BlockSpec(memory_space=pl.ANY),) * 4,
         scratch_shapes=[dma((4, parts))],
-        compiler_params=pltpu.CompilerParams(vmem_limit_bytes=60 * 1024 * 1024),
     )(*results)
 
 

time: 153 us -> 75.1 us (0.49)
  Pallas kernels: 152 us -> 74.3 us
    pallas_call x1, Pallas kernels: 80.7 us -> 3.27 us  [local(): pl.pallas_call(functools.partial(settle, parts), out_shape=(wide, wide, t...]
where the time goes in v3:
time: 75.1 us; the launch traced here: 75 us
  Pallas kernels  74.3 us (99%)
    pallas_call x1, Pallas kernels, local(): pl.pallas_call(functools.partial(kernel, n_seq, n_head, tok), out_shape=(...  71 us
    pallas_call x1, Pallas kernels, local(): pl.pallas_call(functools.partial(settle, parts), out_shape=(wide, wide, t...  3.27 us

profile of v3, /device:TPU:0, one launch (start us, length us, event | category | flops | bytes accessed | tf_op | source)
XLA Modules:
  0.0 75.0 jit_solution(13761977072909155232)
XLA Ops:
  0.6 71.0 %shard_map.84 = (bf16[128,8,4,128]{3,2,1,0:T(4,128)(2,1)}, bf16[128,8,4,128]{3,2,1,0:T(4,128)(2,1)}, bf16[128,8,128]{2,1,0:T(8,128)(2,1)}, bf16[128,8,128]{2,1,0:T(8,128)(2,1)}) custom-call(s32[8]{0:T(128)} %shift_ref.1, bf16[128,8,4,128]{3,2,1,0:T(4,128)(2,1)} %q_ref.1, bf16[128,8,128]{2,1,0:T(8,128)(2,1)} %k_ref.1, bf16[128,8,128]{2,1,0:T(8,128)(2,1)} %v_ref.1, ...), custom_call_target="tpu_custom_call" | custom-call | tf_op jit(solution)/shard_map/pallas_call | solution.py:432
  71.7 3.3 %shard_map.85 = (bf16[128,8,4,128]{3,2,1,0:T(4,128)(2,1)}, bf16[128,8,4,128]{3,2,1,0:T(4,128)(2,1)}, bf16[128,8,128]{2,1,0:T(8,128)(2,1)}, bf16[128,8,128]{2,1,0:T(8,128)(2,1)}) custom-call(bf16[128,8,4,128]{3,2,1,0:T(4,128)(2,1)} %get-tuple-element.8.refs_0_, bf16[128,8,4,128]{3,2,1,0:T(4,128)(2,1)} %get-tuple-element.9.refs_1_, ...), custom_call_target="tpu_custom_call" | custom-call | tf_op jit(solution)/shard_map/pallas_call | solution.py:470

commit v4 on v3

--- a/solution.py
+++ b/solution.py
@@ -27,7 +27,7 @@
     shift_ref, q_ref, k_ref, v_ref, d_ref,
     o_ref, dq_ref, dk_ref, dv_ref,
     kv, part, sib, red, rb_own, rb_far, scores, top8, total8, o_tr, dq_tr, o_buf, dq_buf, fin, k_by, v_by, q_by, d_by, q_by_tr, d_by_tr, perm, inv,
-    own_s, own_r, far_s, far_r, fwd_s, fwd_r, ffwd_s, ffwd_r,
+    own_s, own_r, strip_s, strip_r, far_s, far_r, fwd_s, fwd_r, ffwd_s, ffwd_r,
     sib_s, sib_r, fsib_s, fsib_r, back_s, back_r, fback_s, fback_r,
 ):
     heads = k_ref.shape[1]
@@ -95,27 +95,36 @@
             src_ref=src, dst_ref=dst, send_sem=ssem, recv_sem=rsem, device_id=dev, device_id_type=MESH
         )
 
-    def own_copy(i, to):
-        view = kv.at[i, :, mine, :]
-        return remote(view, view, own_s.at[i, to], own_r.at[i, chip], device(plane, to))
-
-    def own_arrival(i, source):
-        view = kv.at[i, :, pl.ds(pl.multiple_of(HALF + place(source) * tok, tok), tok), :]
-        return remote(view, view, own_s.at[i, source], own_r.at[i, source], device(plane, source))
-
-    def far_copy(i, to):
-        return remote(
-            kv.at[i, :, mine, :],
-            kv.at[i + near, :, pl.ds(pl.multiple_of(pos * tok, tok), tok), :],
-            far_s.at[i, to], far_r.at[i, chip], device(nxt, to),
-        )
-
-    def far_arrival(i, source):
-        view = kv.at[i, :, pl.ds(pl.multiple_of(place(source) * tok, tok), tok), :]
-        return remote(view, view, far_s.at[i - near, source], far_r.at[i - near, source], device(prv, source))
-
     def strip(base, at_pair, parity):
         return pl.ds(pl.multiple_of(base + (at_pair * 2 + parity) * rows, rows), rows)
+
+    def own_copy(i, to_x):
+        view = kv.at[i, :, mine, :]
+        return remote(view, view, own_s.at[i, to_x], own_r.at[i, x], device(plane, y * n_head + to_x))
+
+    def own_arrival(i, from_x):
+        view = kv.at[i, :, pl.ds(pl.multiple_of(HALF + place(y * n_head + from_x) * tok, tok), tok), :]
+        return remote(view, view, own_s.at[i, from_x], own_r.at[i, from_x], device(plane, y * n_head + from_x))
+
+    def strip_copy(i, to_y):
+        view = kv.at[i, :, strip(HALF, y, core), :]
+        return remote(view, view, strip_s.at[i, to_y], strip_r.at[i, y], device(plane, to_y * n_head + x))
+
+    def strip_arrival(i, from_y):
+        view = kv.at[i, :, strip(HALF, from_y, core), :]
+        return remote(view, view, strip_s.at[i, from_y], strip_r.at[i, from_y], device(plane, from_y * n_head + x))
+
+    def far_copy(i, to_y):
+        return remote(
+            kv.at[i, :, strip(HALF, y, core), :], kv.at[i + near, :, strip(0, y, core), :],
+            far_s.at[i, to_y], far_r.at[i, y], device(nxt, to_y * n_head + x),
+        )
+
+    def far_arrival(i, from_y):
+        view = kv.at[i, :, strip(0, from_y, core), :]
+        return remote(
+            view, view, far_s.at[i - near, from_y], far_r.at[i - near, from_y], device(prv, from_y * n_head + x)
+        )
 
     def forward(i, at_pair, parity):
         view = kv.at[i, :, strip(HALF, at_pair, parity), :]
@@ -174,37 +183,42 @@
 
     @pl.loop(0, heads)
     def _(t):
-        i = order(t)
-        for k in range(1, chips):
-            to = (chip + k) % chips
-
-            @pl.when(to // n_head >= y)
-            def _():
-                own_copy(i, to).start()
+        i = t // 2 + (t % 2) * near
+        for k in range(1, n_head):
+            own_copy(i, (x + k) % n_head).start()
+
+    def strip_send(n):
+        i = n // 2 + (n % 2) * near
+        for k in range(1, n_head):
+            own_arrival(i, (x + k) % n_head).wait_recv()
+        for to_y in range(1, pairs):
+
+            @pl.when(to_y > y)
+            def _():
+                strip_copy(i, to_y).start()
+
+        @pl.when(i < near)
+        def _():
+            for to_y in range(pairs):
+                far_copy(i, to_y).start()
+
+    def start_forwards(i):
+        for from_y in range(pairs - 1):
+
+            @pl.when(from_y < y)
+            def _():
+                strip_arrival(i, from_y).wait_recv()
+
+        for at_pair in range(pairs):
+
+            @pl.when(at_pair <= y)
+            def _():
+                forward(i, at_pair, core).start()
 
         @pl.when(i >= near)
         def _():
-            for k in range(chips):
-                far_copy(i - near, (chip + k) % chips).start()
-
-    def start_forwards(i):
-        for k in range(1, chips):
-            source = (chip + k) % chips
-
-            @pl.when(source // n_head <= y)
-            def _():
-                own_arrival(i, source).wait_recv()
-
-        for at_pair in range(pairs):
-
-            @pl.when(at_pair <= y)
-            def _():
-                forward(i, at_pair, core).start()
-
-        @pl.when(i >= near)
-        def _():
-            for k in range(chips):
-                far_arrival(i, (chip + k) % chips).wait_recv()
+            for from_y in range(pairs):
+                far_arrival(i, from_y).wait_recv()
             for at_pair in range(pairs):
                 far_forward(i, at_pair, core).start()
 
@@ -248,9 +262,13 @@
         q_by_tr[i] = q.T
         d_by_tr[i] = d.T
 
-    pl.loop(0, near)(re_lay)
+    @pl.loop(0, 3)
+    def _(n):
+        pl.loop(n * 2, n * 2 + 2)(re_lay)
+        strip_send(n)
+
     start_forwards(0)
-    pl.loop(near, heads)(re_lay)
+    pl.loop(6, heads)(re_lay)
     short = 2 * rows
 
     def blocks(i, step):
@@ -313,6 +331,14 @@
         row_dot = jnp.sum(attended.astype(jnp.float32) * d_by_tr[i].astype(jnp.float32), axis=0, keepdims=True)
         dq_tr[...] = jnp.zeros_like(dq_tr)
 
+        @pl.when(t < 3)
+        def _():
+            strip_send(3 + 2 * t)
+
+        @pl.when(t < 2)
+        def _():
+            strip_send(4 + 2 * t)
+
         @pl.when(t < heads - 1)
         def _():
             start_forwards(order(t + 1))
@@ -374,10 +400,6 @@
         for k in range(1, chips):
             to = (chip + k) % chips
 
-            @pl.when(to // n_head >= y)
-            def _():
-                own_copy(i, to).wait_send()
-
             @pl.when(to // n_head <= y)
             def _():
                 back_copy(i, to).wait_send()
@@ -389,10 +411,18 @@
                 forward(i, at_pair, core).wait_send()
                 sib_copy(i, at_pair).wait_send()
 
+        for k in range(1, n_head):
+            own_copy(i, (x + k) % n_head).wait_send()
+        for to_y in range(1, pairs):
+
+            @pl.when(to_y > y)
+            def _():
+                strip_copy(i, to_y).wait_send()
+
         @pl.when(i < near)
         def _():
-            for k in range(chips):
-                far_copy(i, (chip + k) % chips).wait_send()
+            for to_y in range(pairs):
+                far_copy(i, to_y).wait_send()
 
         @pl.when(i >= near)
         def _():
@@ -457,7 +487,8 @@
             pltpu.VMEM((heads, hd, nq), bf16),
             pltpu.SMEM((heads,), jnp.int32),
             pltpu.SMEM((heads,), jnp.int32),
-            dma((heads, chips)), dma((heads, chips)), dma((near, chips)), dma((near, chips)),
+            dma((heads, n_head)), dma((heads, n_head)), dma((heads, pairs)), dma((heads, pairs)),
+            dma((near, pairs)), dma((near, pairs)),
             dma((heads, pairs)), dma((heads, pairs)), dma((near, pairs)), dma((near, pairs)),
             dma((heads, pairs)), dma((heads, pairs)), dma((near, pairs)), dma((near, pairs)),
             dma((heads, chips)), dma((heads, chips)), dma((near, chips)), dma((near, chips)),

time: 75.1 us -> 88.9 us (1.18)
  Pallas kernels: 74.3 us -> 88.1 us
    pallas_call x1, Pallas kernels: 71 us -> 84.8 us  [local(): pl.pallas_call(functools.partial(kernel, n_seq, n_head, tok), out_shape=(...]
where the time goes in v4:
time: 88.9 us; the launch traced here: 88.7 us
  Pallas kernels  88.1 us (99%)
    pallas_call x1, Pallas kernels, local(): pl.pallas_call(functools.partial(kernel, n_seq, n_head, tok), out_shape=(...  84.8 us
    pallas_call x1, Pallas kernels, local(): pl.pallas_call(functools.partial(settle, parts), out_shape=(wide, wide, t...  3.27 us

profile of v4, /device:TPU:0, one launch (start us, length us, event | category | flops | bytes accessed | tf_op | source)
XLA Modules:
  0.0 88.7 jit_solution(14376990262142525175)
XLA Ops:
  0.6 84.8 %shard_map.84 = (bf16[128,8,4,128]{3,2,1,0:T(4,128)(2,1)}, bf16[128,8,4,128]{3,2,1,0:T(4,128)(2,1)}, bf16[128,8,128]{2,1,0:T(8,128)(2,1)}, bf16[128,8,128]{2,1,0:T(8,128)(2,1)}) custom-call(s32[8]{0:T(128)} %shift_ref.1, bf16[128,8,4,128]{3,2,1,0:T(4,128)(2,1)} %q_ref.1, bf16[128,8,128]{2,1,0:T(8,128)(2,1)} %k_ref.1, bf16[128,8,128]{2,1,0:T(8,128)(2,1)} %v_ref.1, ...), custom_call_target="tpu_custom_call" | custom-call | tf_op jit(solution)/shard_map/pallas_call | solution.py:462
  85.5 3.3 %shard_map.85 = (bf16[128,8,4,128]{3,2,1,0:T(4,128)(2,1)}, bf16[128,8,4,128]{3,2,1,0:T(4,128)(2,1)}, bf16[128,8,128]{2,1,0:T(8,128)(2,1)}, bf16[128,8,128]{2,1,0:T(8,128)(2,1)}) custom-call(bf16[128,8,4,128]{3,2,1,0:T(4,128)(2,1)} %get-tuple-element.8.refs_0_, bf16[128,8,4,128]{3,2,1,0:T(4,128)(2,1)} %get-tuple-element.9.refs_1_, ...), custom_call_target="tpu_custom_call" | custom-call | tf_op jit(solution)/shard_map/pallas_call | solution.py:501

commit v5 on v3

--- a/solution.py
+++ b/solution.py
@@ -10,6 +10,7 @@
 
 GROUP = 2048
 HALF = GROUP // 2
+TILE = 256
 MASKED = -1e30
 MESH = pl.DeviceIdType.MESH
 
@@ -26,7 +27,7 @@
     n_seq, n_head, tok,
     shift_ref, q_ref, k_ref, v_ref, d_ref,
     o_ref, dq_ref, dk_ref, dv_ref,
-    kv, part, sib, red, rb_own, rb_far, scores, top8, total8, o_tr, dq_tr, o_buf, dq_buf, fin, k_by, v_by, q_by, d_by, q_by_tr, d_by_tr, perm, inv,
+    kv, part, sib, red, rb_own, rb_far, scores, narrow, top8, total8, o_tr, dq_tr, o_buf, dq_buf, fin, k_by, v_by, q_by, d_by, q_by_tr, d_by_tr, perm, inv,
     own_s, own_r, far_s, far_r, fwd_s, fwd_r, ffwd_s, ffwd_r,
     sib_s, sib_r, fsib_s, fsib_r, back_s, back_r, fback_s, fback_r,
 ):
@@ -282,14 +283,15 @@
         total8[...] = jnp.zeros_like(total8)
 
         def score_step(start, size):
-            at = pl.ds(start, size)
-            s = nt(kv[i, 0, at, :], q_by_tr[i])
-            if start == HALF:
-                key_at = lax.broadcasted_iota(jnp.int32, (size, nq), 0)
-                query_at = lax.broadcasted_iota(jnp.int32, (1, nq), 1) // per + pos * tok
-                s = jnp.where(key_at <= query_at, s, MASKED)
-            scores[at, :] = s
-            top8[...] = jnp.maximum(top8[...], jnp.max(s.reshape(size // 8, 8, nq), axis=0))
+            for r in range(start, start + size, TILE):
+                at = pl.ds(r, TILE)
+                s = nt(kv[i, 0, at, :], q_by_tr[i])
+                if start == HALF:
+                    key_at = lax.broadcasted_iota(jnp.int32, (TILE, nq), 0) + (r - HALF)
+                    query_at = lax.broadcasted_iota(jnp.int32, (1, nq), 1) // per + pos * tok
+                    s = jnp.where(key_at <= query_at, s, MASKED)
+                scores[at, :] = s
+                top8[...] = jnp.maximum(top8[...], jnp.max(s.reshape(TILE // 8, 8, nq), axis=0))
 
         blocks(i, score_step)
         top = jnp.max(top8[...], axis=0, keepdims=True)
@@ -300,11 +302,14 @@
             pass_on(order(t - 1))
 
         def prob_step(start, size):
+            for r in range(start, start + size, TILE):
+                at = pl.ds(r, TILE)
+                p = jnp.exp2((scores[at, :] - top) * to_exp2)
+                scores[at, :] = p
+                narrow[at, :] = p.astype(jnp.bfloat16)
+                total8[...] += jnp.sum(p.reshape(TILE // 8, 8, nq), axis=0)
             at = pl.ds(start, size)
-            p = jnp.exp2((scores[at, :] - top) * to_exp2)
-            scores[at, :] = p
-            o_tr[...] += tn(kv[i, 1, at, :], p.astype(jnp.bfloat16))
-            total8[...] += jnp.sum(p.reshape(size // 8, 8, nq), axis=0)
+            o_tr[...] += tn(kv[i, 1, at, :], narrow[at, :])
 
         blocks(i, prob_step)
         inverse = 1.0 / jnp.sum(total8[...], axis=0, keepdims=True)
@@ -318,13 +323,15 @@
             start_forwards(order(t + 1))
 
         def grad_step(start, size):
+            for r in range(start, start + size, TILE):
+                at = pl.ds(r, TILE)
+                p = scores[at, :] * inverse
+                ds = (p * (nt(kv[i, 1, at, :], d_by_tr[i]) - row_dot)).astype(jnp.bfloat16)
+                narrow[at, :] = ds
+                part[i, 1, at, :] = nt(p.astype(jnp.bfloat16), d_by[i]).astype(jnp.bfloat16)
+                part[i, 0, at, :] = (nt(ds, q_by[i]) * scaling).astype(jnp.bfloat16)
             at = pl.ds(start, size)
-            k_part = kv[i, 0, at, :]
-            p = scores[at, :] * inverse
-            ds = (p * (nt(kv[i, 1, at, :], d_by_tr[i]) - row_dot)).astype(jnp.bfloat16)
-            part[i, 1, at, :] = nt(p.astype(jnp.bfloat16), d_by[i]).astype(jnp.bfloat16)
-            part[i, 0, at, :] = (nt(ds, q_by[i]) * scaling).astype(jnp.bfloat16)
-            dq_tr[...] += tn(k_part, ds)
+            dq_tr[...] += tn(kv[i, 0, at, :], narrow[at, :])
 
         blocks(i, grad_step)
 
@@ -442,6 +449,7 @@
             pltpu.VMEM((heads, chips, 2, tok, hd), bf16),
             pltpu.VMEM((near, chips, 2, tok, hd), bf16),
             pltpu.VMEM((GROUP, nq), f32),
+            pltpu.VMEM((GROUP, nq), bf16),
             pltpu.VMEM((8, nq), f32),
             pltpu.VMEM((8, nq), f32),
             pltpu.VMEM((hd, nq), f32),

time: 75.1 us -> 75.1 us (level)
  no operation moved by 1% of the time
where the time goes in v5:
time: 75.1 us; the launch traced here: 75 us
  Pallas kernels  74.3 us (99%)
    pallas_call x1, Pallas kernels, local(): pl.pallas_call(functools.partial(kernel, n_seq, n_head, tok), out_shape=(...  71 us
    pallas_call x1, Pallas kernels, local(): pl.pallas_call(functools.partial(settle, parts), out_shape=(wide, wide, t...  3.27 us

profile of v5, /device:TPU:0, one launch (start us, length us, event | category | flops | bytes accessed | tf_op | source)
XLA Modules:
  0.0 75.0 jit_solution(5461023669558161039)
XLA Ops:
  0.6 71.0 %shard_map.84 = (bf16[128,8,4,128]{3,2,1,0:T(4,128)(2,1)}, bf16[128,8,4,128]{3,2,1,0:T(4,128)(2,1)}, bf16[128,8,128]{2,1,0:T(8,128)(2,1)}, bf16[128,8,128]{2,1,0:T(8,128)(2,1)}) custom-call(s32[8]{0:T(128)} %shift_ref.1, bf16[128,8,4,128]{3,2,1,0:T(4,128)(2,1)} %q_ref.1, bf16[128,8,128]{2,1,0:T(8,128)(2,1)} %k_ref.1, bf16[128,8,128]{2,1,0:T(8,128)(2,1)} %v_ref.1, ...), custom_call_target="tpu_custom_call" | custom-call | tf_op jit(solution)/shard_map/pallas_call | solution.py:439
  71.7 3.3 %shard_map.85 = (bf16[128,8,4,128]{3,2,1,0:T(4,128)(2,1)}, bf16[128,8,4,128]{3,2,1,0:T(4,128)(2,1)}, bf16[128,8,128]{2,1,0:T(8,128)(2,1)}, bf16[128,8,128]{2,1,0:T(8,128)(2,1)}) custom-call(bf16[128,8,4,128]{3,2,1,0:T(4,128)(2,1)} %get-tuple-element.8.refs_0_, bf16[128,8,4,128]{3,2,1,0:T(4,128)(2,1)} %get-tuple-element.9.refs_1_, ...), custom_call_target="tpu_custom_call" | custom-call | tf_op jit(solution)/shard_map/pallas_call | solution.py:478
